TPU v7x, 32 devices: a whole 2x2x4 slice. The times are simulated.
32 devices in a mesh: dof: 8 (over z, x), snap: 4 (over y, core).
Axes of the slice: x: 2, y: 2, z: 4, core: 2. Of those that a mesh axis runs over, the one named last changes fastest.
Arguments:
- snapshots: bfloat16 [32768, 1024], P('dof', 'snap')
- lengths: int32 [16], replicated, may hold values from 16 to 64, as said below
- start_block: float32 [1024, 128], replicated, may hold values from -6 to 6
Outputs:
- pod_modes: float32 [32768, 128], P(('dof', 'snap'))
- r_factor: float32 [1024, 1024], replicated
Inputs may be any that keep to these rules, and one draw needn't show every extreme that they name: `lengths`: some passage has all 64 steps active and some passage only a quarter of them.
All inputs are finite; a program needn't handle non-finite values.
Results may differ from a plain program's by a relative error of at most 0.0003.
Values may be sent and summed in bfloat16 or wider, within the bound.
A program may use at most 128 MiB of HBM per device.

v0:
```python
import jax
import jax.numpy as jnp
from jax import lax
from jax.sharding import PartitionSpec as P

STEPS = 64
ITERS = 3
PASSES = 16


def body(snapshots, lengths, start_block):
    panel_width = snapshots.shape[1]
    first_col = lax.axis_index("snap") * panel_width
    columns = first_col + jnp.arange(panel_width, dtype=jnp.int32)
    passage = columns // STEPS
    lookup = passage[:, None] == jnp.arange(PASSES, dtype=jnp.int32)[None, :]
    col_length = jnp.sum(jnp.where(lookup, lengths[None, :], 0), axis=1)
    active = columns % STEPS < col_length
    masked = jnp.where(active[None, :], snapshots, jnp.zeros_like(snapshots))
    gathered_slab = lax.all_gather(masked, "snap", axis=1, tiled=True)
    row_count = gathered_slab.shape[0] * lax.axis_size("dof")
    contract = (((0,), (0,)), ((), ()))
    partial_gram = lax.dot_general(
        gathered_slab, gathered_slab, contract, preferred_element_type=jnp.float32
    )
    gram_sum = lax.psum(partial_gram, "dof")
    width = gram_sum.shape[0]
    shifted = gram_sum / jnp.float32(row_count) + 0.05 * jnp.eye(width, dtype=jnp.float32)
    upper_factor = jnp.linalg.cholesky(shifted).T
    subspace = start_block
    for sweep in range(ITERS):
        image = jnp.dot(
            shifted, subspace, precision=lax.Precision.HIGHEST, preferred_element_type=jnp.float32
        )
        correlation = lax.dot_general(
            image,
            image,
            contract,
            precision=lax.Precision.HIGHEST,
            preferred_element_type=jnp.float32,
        )
        lower_factor = jnp.linalg.cholesky(correlation)
        subspace = lax.linalg.triangular_solve(
            lower_factor, image, left_side=False, lower=True, transpose_a=True
        )
    quarter = gathered_slab.shape[0] // lax.axis_size("snap")
    own_rows = lax.dynamic_slice_in_dim(
        gathered_slab, lax.axis_index("snap") * quarter, quarter, 0
    ).astype(jnp.float32)
    pod_modes = jnp.dot(
        own_rows, subspace, precision=lax.Precision.HIGHEST, preferred_element_type=jnp.float32
    )
    return (pod_modes, upper_factor)


def solution(mesh):
    placed = (P("dof", "snap"), P(), P())
    return jax.shard_map(
        body, mesh=mesh, in_specs=placed, out_specs=(P(("dof", "snap"), None), P()), check_vma=False
    )
```

profile of v0, /device:TPU:0, one launch (start us, length us, event | category | flops | bytes accessed | tf_op | source)
XLA Modules:
  0.0 585.6 jit_solution(14737351477540321371)
XLA Ops:
  11.2 62.2 %all-gather.2.cloned.1.call-done = bf16[4096,1024]{1,0:T(8,128)(2,1)} async-done(((bf16[4096,256]{1,0:T(8,128)(2,1)}), bf16[4096,1024]{1,0:T(8,128)(2,1)}) %all-gather.2.cloned.1.call-update) | async-done | bytes 8388624 | tf_op jit(solution)/shard_map/all_gather | solution.py:20
  73.4 15.0 %fusion.79 = f32[1024,1024]{0,1:T(8,128)} fusion(bf16[4096,1024]{1,0:T(8,128)(2,1)} %all-gather.2.cloned.1.call-done), kind=kOutput, calls=%fused_computation.138 | convolution fusion | flops 8589934592 | bytes 12582912 | tf_op jit(solution)/shard_map/dot_general | solution.py:23
  88.4 156.5 %all-reduce.3.cloned.1.call-done = f32[1024,1024]{0,1:T(8,128)} async-done(((f32[1024,1024]{0,1:T(8,128)}), f32[1024,1024]{0,1:T(8,128)}) %all-reduce.3.cloned.1.call-update) | async-done | bytes 4194320 | tf_op jit(solution)/shard_map/psum | solution.py:26
  262.3 11.7 %cholesky.247 = f32[128,128]{1,0:T(8,128)S(1)} custom-call(f32[128,128]{1,0:T(8,128)S(1)} %cholesky.667), custom_call_target="Cholesky" | custom-call | tf_op jit(solution)/shard_map/jit(cholesky)/cholesky | solution.py:29
  274.1 9.8 %custom-call.64 = f32[1,128,128]{1,2,0:T(8,128)S(1)} custom-call(f32[1,128,128]{2,1,0:T(8,128)S(1)} %get-tuple-element.17), custom_call_target="InvertDiagBlocksLowerTriangular" | custom-call | tf_op jit(solution)/shard_map/jit(cholesky)/cholesky | solution.py:29
  287.3 11.7 %cholesky.270 = f32[128,128]{1,0:T(8,128)S(1)} custom-call(f32[128,128]{1,0:T(8,128)S(1)} %cholesky.671), custom_call_target="Cholesky" | custom-call | tf_op jit(solution)/shard_map/jit(cholesky)/cholesky | solution.py:29
  299.3 9.8 %custom-call.65 = f32[1,128,128]{1,2,0:T(8,128)S(1)} custom-call(f32[1,128,128]{2,1,0:T(8,128)S(1)} %get-tuple-element.15), custom_call_target="InvertDiagBlocksLowerTriangular" | custom-call | tf_op jit(solution)/shard_map/jit(cholesky)/cholesky | solution.py:29
  314.6 11.7 %cholesky.493 = f32[128,128]{1,0:T(8,128)S(1)} custom-call(f32[128,128]{1,0:T(8,128)S(1)} %cholesky.676), custom_call_target="Cholesky" | custom-call | tf_op jit(solution)/shard_map/jit(cholesky)/cholesky | solution.py:29
  327.1 9.8 %custom-call.66 = f32[1,128,128]{1,2,0:T(8,128)S(1)} custom-call(f32[1,128,128]{2,1,0:T(8,128)S(1)} %get-tuple-element.13), custom_call_target="InvertDiagBlocksLowerTriangular" | custom-call | tf_op jit(solution)/shard_map/jit(cholesky)/cholesky | solution.py:29
  341.5 11.7 %cholesky.512 = f32[128,128]{1,0:T(8,128)S(1)} custom-call(f32[128,128]{1,0:T(8,128)S(1)} %cholesky.681), custom_call_target="Cholesky" | custom-call | tf_op jit(solution)/shard_map/jit(cholesky)/cholesky | solution.py:29
  354.0 9.8 %custom-call.67 = f32[1,128,128]{1,2,0:T(8,128)S(1)} custom-call(f32[1,128,128]{2,1,0:T(8,128)S(1)} %get-tuple-element.11), custom_call_target="InvertDiagBlocksLowerTriangular" | custom-call | tf_op jit(solution)/shard_map/jit(cholesky)/cholesky | solution.py:29
  368.1 12.1 %cholesky.531 = f32[128,128]{1,0:T(8,128)S(1)} custom-call(f32[128,128]{1,0:T(8,128)S(1)} %cholesky.686), custom_call_target="Cholesky" | custom-call | tf_op jit(solution)/shard_map/jit(cholesky)/cholesky | solution.py:29
  381.0 9.8 %custom-call.68 = f32[1,128,128]{1,2,0:T(8,128)S(1)} custom-call(f32[1,128,128]{2,1,0:T(8,128)S(1)} %get-tuple-element.9), custom_call_target="InvertDiagBlocksLowerTriangular" | custom-call | tf_op jit(solution)/shard_map/jit(cholesky)/cholesky | solution.py:29
  395.0 11.7 %cholesky.551 = f32[128,128]{1,0:T(8,128)S(1)} custom-call(f32[128,128]{1,0:T(8,128)S(1)} %cholesky.691), custom_call_target="Cholesky" | custom-call | tf_op jit(solution)/shard_map/jit(cholesky)/cholesky | solution.py:29
  407.5 9.8 %custom-call.69 = f32[1,128,128]{1,2,0:T(8,128)S(1)} custom-call(f32[1,128,128]{2,1,0:T(8,128)S(1)} %get-tuple-element.7), custom_call_target="InvertDiagBlocksLowerTriangular" | custom-call | tf_op jit(solution)/shard_map/jit(cholesky)/cholesky | solution.py:29
  421.2 11.7 %cholesky.571 = f32[128,128]{1,0:T(8,128)S(1)} custom-call(f32[128,128]{1,0:T(8,128)S(1)} %cholesky.696), custom_call_target="Cholesky" | custom-call | tf_op jit(solution)/shard_map/jit(cholesky)/cholesky | solution.py:29
  433.7 9.8 %custom-call.70 = f32[1,128,128]{1,2,0:T(8,128)S(1)} custom-call(f32[1,128,128]{2,1,0:T(8,128)S(1)} %get-tuple-element.5), custom_call_target="InvertDiagBlocksLowerTriangular" | custom-call | tf_op jit(solution)/shard_map/jit(cholesky)/cholesky | solution.py:29
  446.5 11.7 %cholesky.589 = f32[128,128]{1,0:T(8,128)S(1)} custom-call(f32[128,128]{1,0:T(8,128)S(1)} %convolution_subtract_fusion.6), custom_call_target="Cholesky" | custom-call | tf_op jit(solution)/shard_map/jit(cholesky)/cholesky | solution.py:29
  468.5 11.7 %cholesky.636 = f32[128,128]{1,0:T(8,128)S(1)} custom-call(f32[128,128]{1,0:T(8,128)S(1)} %fusion.38), custom_call_target="Cholesky" | custom-call | tf_op jit(solution)/shard_map/jit(cholesky)/cholesky | solution.py:42
  481.6 9.8 %custom-call.73 = f32[1,128,128]{1,2,0:T(8,128)S(1)} custom-call(f32[1,128,128]{2,1,0:T(8,128)S(1)} %fusion.21), custom_call_target="InvertDiagBlocksLowerTriangular" | custom-call | tf_op jit(solution)/shard_map/triangular_solve/custom-call.16 | solution.py:43
  502.4 11.7 %cholesky.647 = f32[128,128]{1,0:T(8,128)S(1)} custom-call(f32[128,128]{1,0:T(8,128)S(1)} %fusion.36), custom_call_target="Cholesky" | custom-call | tf_op jit(solution)/shard_map/jit(cholesky)/cholesky | solution.py:42
  515.5 9.8 %custom-call.74 = f32[1,128,128]{1,2,0:T(8,128)S(1)} custom-call(f32[1,128,128]{2,1,0:T(8,128)S(1)} %fusion.22), custom_call_target="InvertDiagBlocksLowerTriangular" | custom-call | tf_op jit(solution)/shard_map/triangular_solve/custom-call.16 | solution.py:43
  536.0 11.7 %cholesky.658 = f32[128,128]{1,0:T(8,128)S(1)} custom-call(f32[128,128]{1,0:T(8,128)S(1)} %fusion.34), custom_call_target="Cholesky" | custom-call | tf_op jit(solution)/shard_map/jit(cholesky)/cholesky | solution.py:42
  549.1 9.8 %custom-call.75 = f32[1,128,128]{1,2,0:T(8,128)S(1)} custom-call(f32[1,128,128]{2,1,0:T(8,128)S(1)} %fusion.23), custom_call_target="InvertDiagBlocksLowerTriangular" | custom-call | tf_op jit(solution)/shard_map/triangular_solve/custom-call.16 | solution.py:43
  (97 shorter events, 105.1 us)
Async XLA Ops:
  7.2 451.2 %copy-start = (f32[1024,128]{1,0:T(8,128)S(1)}, f32[1024,128]{1,0:T(8,128)}, u32[]{:S(2)}) copy-start(f32[1024,128]{1,0:T(8,128)} %param.8) | copy-start | bytes 1572868
  7.2 66.2 %all-gather.2.cloned.1.call-start = ((), (), s32[]{:S(2)}) async-start(), calls=%async_computation | async-start | bytes 10485760 | tf_op jit(solution)/shard_map/all_gather | solution.py:20
  11.1 233.8 %all-reduce.3.cloned.1.call-start = ((), (), s32[]{:S(2)}) async-start(), calls=%async_computation.1 | async-start | bytes 8388608 | tf_op jit(solution)/shard_map/psum | solution.py:26
  260.3 2.0 copy-start.2
  310.2 2.0 copy-start.1
Sparse Core Ops, SparseCore 0:
  11.2 62.0 all-gather.1
  88.6 156.2 all-reduce.2
where the time goes:
time: 591 us; the launch traced here: 586 us
  other arithmetic  254 us (43%)
  waiting for transfers between devices  219 us (37%)
  matrix products  77.3 us (13%)
  between operations  19.6 us (3%)
  local copies, waits for them, and re-layouts  15.6 us (3%)
    another operation x30, other arithmetic, body(): upper_factor = jnp.linalg.cholesky(shifted).T  167 us
    psum x1, waiting for transfers between devices, body(): gram_sum = lax.psum(partial_gram, 'dof')  156 us
    all_gather x1, waiting for transfers between devices, body(): gathered_slab = lax.all_gather(masked, 'snap', axis=1, tiled=True)  62.2 us
    another operation x9, other arithmetic, body(): lower_factor = jnp.linalg.cholesky(correlation)  37.2 us
    another operation x6, other arithmetic, body(): lax.linalg.triangular_solve(lower_factor, image, left_side=False, lower=T...  31.4 us
    dot_general x3, matrix products, body(): jnp.dot(shifted, subspace, precision=lax.Precision.HIGHEST, preferred_ele...  27.2 us
    another operation x14, matrix products, body(): upper_factor = jnp.linalg.cholesky(shifted).T  25.9 us
    dot_general x1, matrix products, body(): lax.dot_general(gathered_slab, gathered_slab, contract, preferred_element...  15 us
  transfers between devices with their start and end apart: 2, of which 2 were waited for; matrix products, arithmetic and copies ran while one was open for 0% of the time, Pallas kernels for 0%

commit v1 on v0

v1 whole, which is shorter than its diff:
```python
import functools

import jax
import jax.numpy as jnp
from jax import lax
from jax.experimental import pallas as pl
from jax.experimental.pallas import tpu as pltpu
from jax.sharding import PartitionSpec as P

STEPS = 64
ITERS = 3
PASSES = 16
B = 128
VMEM_LIMIT = 48 * 1024 * 1024
F32 = jnp.float32
BF16 = jnp.bfloat16
COL0 = (((0,), (0,)), ((), ()))
ROWCOL = (((1,), (0,)), ((), ()))
COLCOL = (((1,), (1,)), ((), ()))


def split3(x):
    hi = x.astype(BF16)
    rest = x - hi.astype(F32)
    mid = rest.astype(BF16)
    low = (rest - mid.astype(F32)).astype(BF16)
    return hi, mid, low


def dot6(a, b, dims):
    return lax.dot_general(
        a, b, dims, precision=lax.Precision.HIGHEST, preferred_element_type=F32
    )


def factor_block(block):
    rows = [None] * (B // 8)
    for i in range(B // 8):
        r = lax.broadcasted_iota(jnp.int32, (8, B), 0) + 8 * i
        c = lax.broadcasted_iota(jnp.int32, (8, B), 1)
        rows[i] = (block[8 * i : 8 * i + 8, :], jnp.where(r == c, 1.0, 0.0).astype(F32))
    sub = lax.broadcasted_iota(jnp.int32, (8, B), 0)
    upper, inverse = [], []
    for g in range(B // 8):
        left, right = rows[g]
        cols = [
            jnp.broadcast_to(left[:, 8 * g + t : 8 * g + t + 1], (8, B)) for t in range(8)
        ]
        outer = [
            [
                jnp.broadcast_to(rows[i][0][:, 8 * g + t : 8 * g + t + 1], (8, B))
                for t in range(8)
            ]
            for i in range(g + 1, B // 8)
        ]
        u_tile = jnp.zeros((8, B), F32)
        v_tile = jnp.zeros((8, B), F32)
        for t in range(8):
            pivot = jnp.broadcast_to(cols[t][t : t + 1, :], (8, B))
            recip = 1.0 / pivot
            scale = lax.rsqrt(pivot)
            left_row = jnp.broadcast_to(left[t : t + 1, :], (8, B))
            right_row = jnp.broadcast_to(right[t : t + 1, :], (8, B))
            u_tile = jnp.where(sub == t, left_row * scale, u_tile)
            v_tile = jnp.where(sub == t, right_row * scale, v_tile)
            factor = jnp.where(sub == t, cols[t] - 1.0, cols[t]) * recip
            left_new = jnp.where(sub == t, left_row * recip, left - factor * left_row)
            right_new = jnp.where(sub == t, right_row * recip, right - factor * right_row)
            for c in range(t + 1, 8):
                head = jnp.broadcast_to(cols[c][t : t + 1, :], (8, B))
                cols[c] = jnp.where(sub == t, head * recip, cols[c] - factor * head)
            left, right = left_new, right_new
        upper.append(u_tile)
        inverse.append(v_tile)
        left_rows = [jnp.broadcast_to(left[t : t + 1, :], (8, B)) for t in range(8)]
        right_rows = [jnp.broadcast_to(right[t : t + 1, :], (8, B)) for t in range(8)]
        for i in range(g + 1, B // 8):
            a, b = rows[i]
            coef = outer[i - g - 1]
            for t in range(8):
                a = a - coef[t] * left_rows[t]
                b = b - coef[t] * right_rows[t]
            rows[i] = (a, b)
    u = jnp.concatenate(upper, axis=0)
    v = jnp.concatenate(inverse, axis=0)
    r = lax.broadcasted_iota(jnp.int32, (B, B), 0)
    c = lax.broadcasted_iota(jnp.int32, (B, B), 1)
    return jnp.where(c >= r, u, 0.0), v


def cholesky_kernel(a_ref, r_ref, left_ref, right_ref, diag_ref, inv_ref):
    width = a_ref.shape[0]
    count = width // B
    r_ref[...] = a_ref[...]

    @pl.loop(0, count)
    def panel(k):
        here = pl.ds(pl.multiple_of(k * B, B), B)
        u, v = factor_block(r_ref[here, here])
        row = dot6(v, r_ref[here, :], ROWCOL)
        col = lax.broadcasted_iota(jnp.int32, (B, width), 1)
        row = jnp.where(col >= (k + 1) * B, row, 0.0)
        r_ref[here, :] = row
        r_ref[here, here] = u
        hi, mid, low = split3(row)
        left_ref[...] = jnp.concatenate([hi, mid, hi, low, mid, hi], axis=0)
        right_ref[...] = jnp.concatenate([hi, hi, mid, hi, mid, low], axis=0)

        @pl.loop(k + 1, count)
        def update(i):
            there = pl.ds(pl.multiple_of(i * B, B), B)
            r_ref[there, :] = r_ref[there, :] - lax.dot_general(
                left_ref[:, there], right_ref[...], COL0, preferred_element_type=F32
            )


def cholesky(shifted):
    width = shifted.shape[0]
    return pl.pallas_call(
        cholesky_kernel,
        out_shape=jax.ShapeDtypeStruct((width, width), F32),
        in_specs=[pl.BlockSpec(memory_space=pltpu.VMEM)],
        out_specs=pl.BlockSpec(memory_space=pltpu.VMEM),
        scratch_shapes=[
            pltpu.VMEM((6 * B, width), BF16),
            pltpu.VMEM((6 * B, width), BF16),
            pltpu.VMEM((B, B), F32),
            pltpu.VMEM((B, B), F32),
        ],
        compiler_params=pltpu.CompilerParams(vmem_limit_bytes=VMEM_LIMIT),
        name="cholesky",
    )(shifted)


def iterate_kernel(a_ref, x_ref, o_ref, hi_ref, mid_ref, low_ref):
    width, modes = x_ref.shape
    hi_ref[...], mid_ref[...], low_ref[...] = split3(a_ref[...])
    o_ref[...] = x_ref[...]

    @pl.loop(0, ITERS)
    def sweep(_):
        x1, x2, x3 = split3(o_ref[...])
        first = lax.dot_general(
            hi_ref[...],
            jnp.concatenate([x1, x2, x3], axis=1),
            ROWCOL,
            preferred_element_type=F32,
        )
        second = lax.dot_general(
            mid_ref[...],
            jnp.concatenate([x1, x2], axis=1),
            ROWCOL,
            preferred_element_type=F32,
        )
        third = lax.dot_general(low_ref[...], x1, ROWCOL, preferred_element_type=F32)
        image = (
            (third + second[:, modes:] + first[:, 2 * modes :])
            + (first[:, modes : 2 * modes] + second[:, :modes])
            + first[:, :modes]
        )
        correlation = dot6(image, image, COL0)
        _, v = factor_block(correlation)
        o_ref[...] = dot6(image, v, COLCOL)


def iterate(shifted, start_block):
    width, modes = start_block.shape
    return pl.pallas_call(
        iterate_kernel,
        out_shape=jax.ShapeDtypeStruct((width, modes), F32),
        in_specs=[pl.BlockSpec(memory_space=pltpu.VMEM)] * 2,
        out_specs=pl.BlockSpec(memory_space=pltpu.VMEM),
        scratch_shapes=[pltpu.VMEM((width, width), BF16)] * 3,
        compiler_params=pltpu.CompilerParams(vmem_limit_bytes=VMEM_LIMIT),
        name="iterate",
    )(shifted, start_block)


def modes_kernel(m_ref, b_ref, o_ref):
    modes = b_ref.shape[1]
    b1, b2, b3 = split3(b_ref[...])
    parts = lax.dot_general(
        m_ref[...], jnp.concatenate([b1, b2, b3], axis=1), ROWCOL, preferred_element_type=F32
    )
    o_ref[...] = (parts[:, 2 * modes :] + parts[:, modes : 2 * modes]) + parts[:, :modes]


def modes_of(masked, block):
    return pl.pallas_call(
        modes_kernel,
        out_shape=jax.ShapeDtypeStruct((masked.shape[0], block.shape[1]), F32),
        in_specs=[pl.BlockSpec(memory_space=pltpu.VMEM)] * 2,
        out_specs=pl.BlockSpec(memory_space=pltpu.VMEM),
        compiler_params=pltpu.CompilerParams(vmem_limit_bytes=VMEM_LIMIT),
        name="modes",
    )(masked, block)


def active_columns(lengths, width):
    columns = jnp.arange(width, dtype=jnp.int32)
    lookup = (columns // STEPS)[:, None] == jnp.arange(PASSES, dtype=jnp.int32)[None, :]
    col_length = jnp.sum(jnp.where(lookup, lengths[None, :], 0), axis=1)
    return columns % STEPS < col_length


def body(snapshots, lengths, start_block):
    snap = lax.axis_size("snap")
    width = start_block.shape[0]
    row_count = snapshots.shape[0] * lax.axis_size("dof")
    own = lax.all_to_all(snapshots, "snap", split_axis=0, concat_axis=1, tiled=True)
    active = active_columns(lengths, width)
    masked = jnp.where(active[None, :], own, jnp.zeros_like(own))
    gram = lax.psum(
        lax.dot_general(masked, masked, COL0, preferred_element_type=F32), ("dof", "snap")
    )
    shifted = gram / F32(row_count) + 0.05 * jnp.eye(width, dtype=F32)
    first = lax.axis_index("snap") % 2 == 0
    upper, block = lax.cond(
        first,
        lambda: (cholesky(shifted), start_block),
        lambda: (shifted, iterate(shifted, start_block)),
    )
    down = [(i, i + 1) for i in range(0, snap, 2)]
    up = [(i + 1, i) for i in range(0, snap, 2)]
    upper = jnp.where(first, upper, lax.ppermute(upper, "snap", down))
    block = jnp.where(first, lax.ppermute(block, "snap", up), block)
    return modes_of(masked, block), upper


def solution(mesh):
    placed = (P("dof", "snap"), P(), P())
    return jax.shard_map(
        body, mesh=mesh, in_specs=placed, out_specs=(P(("dof", "snap"), None), P()), check_vma=False
    )
```

time: 591 us -> 267 us (0.45)
  other arithmetic: 254 us -> 8.54 us
  matrix products: 77.3 us -> 4.38 us
  Pallas kernels: 0 us -> 58.2 us
  waiting for transfers between devices: 219 us -> 171 us
  local copies, waits for them, and re-layouts: 15.6 us -> 3.27 us
  starting transfers between devices: 0.08 us -> 7.1 us
    another operation x45 -> x0, other arithmetic: 236 us -> none  [the longest x30 167 us: body(): upper_factor = jnp.linalg.cholesky(shifted).T]
    all_gather x1 -> x0, waiting for transfers between devices: 62.2 us -> none  [body(): gathered_slab = lax.all_gather(masked, 'snap', axis=1, tiled=True)]
    pallas_call x0 -> x2, Pallas kernels: none -> 58.2 us  [the longest x1 56.1 us: cholesky(): pl.pallas_call(cholesky_kernel, out_shape=jax.ShapeDtypeStruct((width, wi...]
    dot_general x8 -> x1, matrix products: 49.5 us -> 4.38 us  [body(): lax.dot_general(masked, masked, COL0, preferred_element_type=F32)]
    another operation x17 -> x0, matrix products: 27.9 us -> none  [the longest x14 25.9 us: body(): upper_factor = jnp.linalg.cholesky(shifted).T]
    all_to_all x0 -> x1, waiting for transfers between devices: none -> 25.6 us  [body(): lax.all_to_all(snapshots, 'snap', split_axis=0, concat_axis=1, tiled=True)]
    psum x1, waiting for transfers between devices: 156 us -> 143 us  [body(): lax.psum(lax.dot_general(masked, masked, COL0, preferred_element_type=F32...]
  transfers between devices with their start and end apart: 2 -> 4, of which waited for: 2 -> 4; matrix products, arithmetic and copies ran while one was open for 0% -> 0% of each run, Pallas kernels for 0% -> 1%
where the time goes in v1:
time: 267 us
  waiting for transfers between devices  171 us (64%)
  Pallas kernels  58.2 us (22%)
  between operations  14.1 us (5%)
  other arithmetic  8.54 us (3%)
  starting transfers between devices  7.1 us (3%)
  matrix products  4.38 us (2%)
  local copies, waits for them, and re-layouts  3.27 us (1%)
    psum x1, waiting for transfers between devices, body(): lax.psum(lax.dot_general(masked, masked, COL0, preferred_element_type=F32...  143 us
    pallas_call x1, Pallas kernels, cholesky(): pl.pallas_call(cholesky_kernel, out_shape=jax.ShapeDtypeStruct((width, wi...  56.1 us
    all_to_all x1, waiting for transfers between devices, body(): lax.all_to_all(snapshots, 'snap', split_axis=0, concat_axis=1, tiled=True)  25.6 us
  transfers between devices with their start and end apart: 4, of which 4 were waited for; matrix products, arithmetic and copies ran while one was open for 0% of the time, Pallas kernels for 1%

profile of v1, /device:TPU:0, one launch (start us, length us, event | category | flops | bytes accessed | tf_op | source)
XLA Modules:
  0.0 267.0 jit_solution(6747991355550067788)
XLA Ops:
  7.2 0.0 copy-start.1
  7.2 4.2 %all-to-all-start = ((bf16[4,1024,256]{2,1,0:T(8,128)(2,1)}), bf16[4,1024,256]{2,1,0:T(8,128)(2,1)S(1)}, u32[]{:S(2)}, u32[]{:S(2)}) async-start(bf16[4,1024,256]{2,1,0:T(8,128)(2,1)} %bitcast.12), calls=%async_computation | async-start | bytes 4194304 | tf_op jit(solution)/shard_map/all_to_all | solution.py:210
  11.4 0.0 all-reduce.2.cloned.1.call-start
  11.4 0.1 select_reduce_fusion
  11.6 25.6 %all-to-all-done = bf16[4,1024,256]{2,1,0:T(8,128)(2,1)S(1)} async-done(((bf16[4,1024,256]{2,1,0:T(8,128)(2,1)}), bf16[4,1024,256]{2,1,0:T(8,128)(2,1)S(1)}, u32[]{:S(2)}, u32[]{:S(2)}) %all-to-all-start) | async-done | bytes 2097184 | tf_op jit(solution)/shard_map/all_to_all | solution.py:210
  37.1 2.4 copy.9
  39.5 1.8 bitcast_select_fusion
  41.3 4.4 %fusion.10 = f32[1024,1024]{1,0:T(8,128)} fusion(bf16[1024,1024]{0,1:T(8,128)(2,1)S(1)} %bitcast.11), kind=kOutput, calls=%fused_computation.25 | convolution fusion | flops 2147483648 | bytes 6291456 | tf_op jit(solution)/shard_map/dot_general | solution.py:214
  45.7 0.0 all-reduce.2.cloned.1.call-update
  45.7 0.0 copy-start
  45.7 143.0 %all-reduce.2.cloned.1.call-done = f32[1024,1024]{1,0:T(8,128)} async-done(((f32[1024,1024]{1,0:T(8,128)}), f32[1024,1024]{1,0:T(8,128)}) %all-reduce.2.cloned.1.call-update) | async-done | bytes 4194320 | tf_op jit(solution)/shard_map/psum | solution.py:213
  188.7 3.0 %select_add_fusion = f32[1024,1024]{1,0:T(8,128)S(1)} fusion(f32[1024,1024]{1,0:T(8,128)} %all-reduce.2.cloned.1.call-done), kind=kLoop, calls=%fused_computation | loop fusion | flops 4194304 | bytes 8388608 | tf_op jit(solution)/shard_map/add | solution.py:216
  191.8 57.0 %conditional.1 = (f32[1024,1024]{1,0:T(8,128)S(1)}, f32[1024,128]{1,0:T(8,128)S(1)}) conditional(s32[]{:T(128)} %convert_element_type.4, (f32[1024,1024]{1,0:T(8,128)S(1)}, f32[1024,128]{1,0:T(8,128)S(1)}) %tuple.22, (f32[1024,1024]{1,0:T(8,128)S(1)}, f32[1024,128]{1,0:T(8,128)S(1)}) %tuple.23), branch_computations={%region_2.3_spmd, %region_3.4_spmd} | conditional | bytes 9437200 | solution.py:218
  192.0 0.6 copy.19.a_ref
  192.6 56.1 %cholesky.1 = f32[1024,1024]{1,0:T(8,128)S(1)} custom-call(f32[1024,1024]{1,0:T(8,128)S(1)} %copy.19.a_ref), custom_call_target="tpu_custom_call" | custom-call | tf_op jit(solution)/shard_map/cond/branch_1_fun/cholesky/pallas_call | solution.py:119
  248.7 1.6 collective-permute-start.1
  250.3 1.3 collective-permute-start
  251.6 0.3 copy.12
  251.9 0.1 broadcast_select_fusion.1.m_ref
  252.1 2.1 collective-permute-done
  254.1 0.1 broadcast_select_fusion.2.b_ref
  254.2 2.1 modes.1
  256.2 0.6 collective-permute-done.1
  256.8 3.4 %broadcast_select_fusion = f32[1024,1024]{1,0:T(8,128)} fusion(f32[1024,1024]{1,0:T(8,128)S(1)} %get-tuple-element.17, f32[1024,1024]{1,0:T(8,128)S(1)} %collective-permute-done.1, pred[]{:T(512)S(6)} %eq.26), kind=kLoop, calls=%fused_computation.3 | loop fusion | flops 1048576 | bytes 12582913 | tf_op jit(solution)/shard_map/jit(_where)/select_n | solution.py:225
  (7 shorter events, 0.1 us)
Async XLA Ops:
  7.2 4.3 %copy-start.1 = (s32[16]{0:T(128)S(1)}, s32[16]{0:T(128)}, u32[]{:S(2)}) copy-start(s32[16]{0:T(128)} %param.6) | copy-start | bytes 196
  7.2 29.9 %all-to-all-start = ((bf16[4,1024,256]{2,1,0:T(8,128)(2,1)}), bf16[4,1024,256]{2,1,0:T(8,128)(2,1)S(1)}, u32[]{:S(2)}, u32[]{:S(2)}) async-start(bf16[4,1024,256]{2,1,0:T(8,128)(2,1)} %bitcast.12), calls=%async_computation | async-start | bytes 4194304 | tf_op jit(solution)/shard_map/all_to_all | solution.py:210
  11.4 177.3 %all-reduce.2.cloned.1.call-start = ((), (), s32[]{:S(2)}) async-start(), calls=%async_computation.1 | async-start | bytes 8388608 | tf_op jit(solution)/shard_map/psum | solution.py:213
  45.7 146.1 %copy-start = (f32[1024,128]{1,0:T(8,128)S(1)}, f32[1024,128]{1,0:T(8,128)}, u32[]{:S(2)}) copy-start(f32[1024,128]{1,0:T(8,128)} %param.7) | copy-start | bytes 1572868
  248.7 8.1 %collective-permute-start.1 = (f32[1024,1024]{1,0:T(8,128)S(1)}, f32[1024,1024]{1,0:T(8,128)S(1)}, u32[]{:S(2)}, u32[]{:S(2)}) collective-permute-start(f32[1024,1024]{1,0:T(8,128)S(1)} %get-tuple-element.17), channel_id=1, source_target_pairs={{0,1},{2,3},{4,5},{6,7},{8,9},{10,11},{12,13},{14,15},{16,17},{18,... | collective-permute-start | bytes 12582920 | tf_op jit(solution)/shard_map/ppermute | solution.py:225
  250.3 3.8 %collective-permute-start = (f32[1024,128]{1,0:T(8,128)S(1)}, f32[1024,128]{1,0:T(8,128)S(1)}, u32[]{:S(2)}, u32[]{:S(2)}) collective-permute-start(f32[1024,128]{1,0:T(8,128)S(1)} %get-tuple-element.16), channel_id=1, source_target_pairs={{1,0},{3,2},{5,4},{7,6},{9,8},{11,10},{13,12},{15,14},{17,16},{19,... | collective-permute-start | bytes 1572872 | tf_op jit(solution)/shard_map/ppermute | solution.py:226
Sparse Core Ops, SparseCore 0:
  45.8 142.8 all-reduce.1

commit v2 on v1

--- a/solution.py
+++ b/solution.py
@@ -88,10 +88,250 @@
     return jnp.where(c >= r, u, 0.0), v
 
 
-def cholesky_kernel(a_ref, r_ref, left_ref, right_ref, diag_ref, inv_ref):
-    width = a_ref.shape[0]
+MESH = pl.DeviceIdType.MESH
+
+
+def block_rows(i, j, count):
+    return (i * count - i * (i - 1) // 2 + (j - i)) * B
+
+
+def packed_rows(count, devices):
+    chunk = -(-(count * (count + 1) // 2 * B) // (8 * devices)) * 8
+    return chunk * devices
+
+
+def stages_of(dofs, snaps):
+    d, s = lax.axis_index("dof"), lax.axis_index("snap")
+    core, x, y = s % 2, d % 2, (s // 2) % 2
+    stages = [(core, 2, lambda j: (d, s + 1 - 2 * core))]
+    rest = 1 - core
+    if snaps == 4 and dofs % 2 == 0:
+        stages.append(
+            (
+                rest * x + core * y,
+                2,
+                lambda j: (d + rest * (1 - 2 * x), s + core * 2 * (1 - 2 * y)),
+            )
+        )
+        stages.append(
+            (
+                rest * y + core * x,
+                2,
+                lambda j: (d + core * (1 - 2 * x), s + rest * 2 * (1 - 2 * y)),
+            )
+        )
+        stride = 2
+    else:
+        wide = snaps // 2
+        if wide > 1:
+            high = s // 2
+            stages.append((high, wide, lambda j: (d, s + 2 * ((high + j) % wide - high))))
+        stride = 1
+    while stride < dofs:
+        left = dofs // stride
+        radix = 4 if left % 4 == 0 else 2 if left % 2 == 0 else left
+        digit = (d // stride) % radix
+        stages.append(
+            (
+                digit,
+                radix,
+                lambda j, g=digit, r=radix, t=stride: (d + t * ((g + j) % r - g), s),
+            )
+        )
+        stride *= radix
+    return stages
+
+
+def gram_kernel(
+    dofs, snaps, x_ref, active_ref, m_ref, g_ref, slots, part, total, *rest
+):
+    landing, sems = rest[:-4], rest[-4:]
+    swap_sems, own_sem, send_sems, recv_sems = sems
+    d, s = lax.axis_index("dof"), lax.axis_index("snap")
+    stages = stages_of(dofs, snaps)
+    rows, panel = slots.shape[1], slots.shape[2]
+    width = m_ref.shape[1]
     count = width // B
-    r_ref[...] = a_ref[...]
+
+    peers = [(d, (s + j) % snaps) for j in range(1, snaps)]
+    barrier = pltpu.get_barrier_semaphore()
+    if snaps == 4 and dofs % 2 == 0:
+        greet = list(peers) + [(d + 1 - 2 * (d % 2), s)]
+        for _, radix, peer in stages[3:]:
+            greet += [peer(j) for j in range(1, radix)]
+    else:
+        greet = list(peers)
+        for _, radix, peer in stages[1 + (snaps > 2) :]:
+            greet += [peer(j) for j in range(1, radix)]
+    for device in greet:
+        pl.semaphore_signal(barrier, inc=1, device_id=device, device_id_type=MESH)
+    pl.semaphore_wait(barrier, len(greet))
+
+    swaps = []
+    for j in range(1, snaps):
+        target = (s + j) % snaps
+        copy = pltpu.make_async_remote_copy(
+            src_ref=x_ref.at[pl.ds(pl.multiple_of(target * rows, 16), rows), :],
+            dst_ref=slots.at[s],
+            send_sem=swap_sems.at[0, j],
+            recv_sem=swap_sems.at[1, j],
+            device_id=(d, target),
+            device_id_type=MESH,
+        )
+        copy.start()
+        swaps.append(copy)
+    own = pltpu.make_async_copy(
+        x_ref.at[pl.ds(pl.multiple_of(s * rows, 16), rows), :], slots.at[s], own_sem
+    )
+    own.start()
+    own.wait()
+    for copy in swaps:
+        copy.wait_recv()
+    for i in range(snaps):
+        columns = slice(i * panel, (i + 1) * panel)
+        m_ref[:, columns] = (
+            slots[i].astype(F32) * active_ref[0:1, columns]
+        ).astype(BF16)
+
+    for i in range(count):
+        strip = lax.dot_general(
+            m_ref[:, i * B : (i + 1) * B],
+            m_ref[:, i * B :],
+            COL0,
+            preferred_element_type=F32,
+        )
+        for j in range(i, count):
+            first = block_rows(i, j, count)
+            part[first : first + B, :] = strip[:, (j - i) * B : (j - i + 1) * B]
+    end = block_rows(count - 1, count - 1, count) + B
+    if end < part.shape[0]:
+        part[end:, :] = jnp.zeros((part.shape[0] - end, B), F32)
+    for copy in swaps:
+        copy.wait_send()
+
+    offset, length = 0, part.shape[0]
+    spans = []
+    for n, (digit, radix, peer) in enumerate(stages):
+        size = length // radix
+        copies = []
+        for j in range(1, radix):
+            there = offset + ((digit + j) % radix) * size
+            copy = pltpu.make_async_remote_copy(
+                src_ref=part.at[pl.ds(pl.multiple_of(there, 8), size), :],
+                dst_ref=landing[n].at[j - 1],
+                send_sem=send_sems.at[0, n, j],
+                recv_sem=recv_sems.at[0, n, j],
+                device_id=peer(j),
+                device_id_type=MESH,
+            )
+            copy.start()
+            copies.append(copy)
+        offset = offset + digit * size
+        length = size
+        spans.append((offset, size))
+        here = pl.ds(pl.multiple_of(offset, 8), size)
+        for copy in copies:
+            copy.wait_recv()
+        value = part[here, :]
+        for j in range(1, radix):
+            value = value + landing[n][j - 1]
+        if n == len(stages) - 1:
+            total[here, :] = value
+        else:
+            part[here, :] = value
+        for copy in copies:
+            copy.wait_send()
+
+    for n in reversed(range(len(stages))):
+        _, radix, peer = stages[n]
+        start, size = spans[n]
+        here = pl.ds(pl.multiple_of(start, 8), size)
+        copies = []
+        for j in range(1, radix):
+            copy = pltpu.make_async_remote_copy(
+                src_ref=total.at[here, :],
+                dst_ref=total.at[here, :],
+                send_sem=send_sems.at[1, n, j],
+                recv_sem=recv_sems.at[1, n, j],
+                device_id=peer(j),
+                device_id_type=MESH,
+            )
+            copy.start()
+            copies.append(copy)
+        for copy in copies:
+            copy.wait_recv()
+        for copy in copies:
+            copy.wait_send()
+    g_ref[...] = total[...]
+
+
+def gram_of(snapshots, active, dofs, snaps):
+    rows, panel = snapshots.shape[0] // snaps, snapshots.shape[1]
+    width = panel * snaps
+    packed = packed_rows(width // B, dofs * snaps)
+    radices = [2]
+    if snaps == 4 and dofs % 2 == 0:
+        radices += [2, 2]
+        stride = 2
+    else:
+        radices += [snaps // 2] if snaps > 2 else []
+        stride = 1
+    while stride < dofs:
+        left = dofs // stride
+        radices.append(4 if left % 4 == 0 else 2 if left % 2 == 0 else left)
+        stride *= radices[-1]
+    landing, length = [], packed
+    for radix in radices:
+        length //= radix
+        landing.append(pltpu.VMEM((radix - 1, length, B), F32))
+    most = max(radices)
+    return pl.pallas_call(
+        functools.partial(gram_kernel, dofs, snaps),
+        out_shape=(
+            jax.ShapeDtypeStruct((rows, width), BF16),
+            jax.ShapeDtypeStruct((packed, B), F32),
+        ),
+        in_specs=[
+            pl.BlockSpec(memory_space=pl.ANY),
+            pl.BlockSpec(memory_space=pltpu.VMEM),
+        ],
+        out_specs=(pl.BlockSpec(memory_space=pltpu.VMEM),) * 2,
+        scratch_shapes=[
+            pltpu.VMEM((snaps, rows, panel), BF16),
+            pltpu.VMEM((packed, B), F32),
+            pltpu.VMEM((packed, B), F32),
+            *landing,
+            pltpu.SemaphoreType.DMA((2, snaps)),
+            pltpu.SemaphoreType.DMA,
+            pltpu.SemaphoreType.DMA((2, len(radices), most)),
+            pltpu.SemaphoreType.DMA((2, len(radices), most)),
+        ],
+        compiler_params=pltpu.CompilerParams(
+            collective_id=0, has_side_effects=True, vmem_limit_bytes=VMEM_LIMIT
+        ),
+        name="gram",
+    )(snapshots, active)
+
+
+def shifted_block(g_ref, i, j, count, row_count):
+    first = block_rows(i, j, count)
+    block = g_ref[first : first + B, :] / F32(row_count)
+    if i == j:
+        r = lax.broadcasted_iota(jnp.int32, (B, B), 0)
+        c = lax.broadcasted_iota(jnp.int32, (B, B), 1)
+        block = block + jnp.where(r == c, 0.05, 0.0).astype(F32)
+    return block
+
+
+def cholesky_kernel(row_count, g_ref, r_ref, left_ref, right_ref):
+    width = r_ref.shape[0]
+    count = width // B
+    for i in range(count):
+        r_ref[i * B : (i + 1) * B, :] = jnp.zeros((B, width), F32)
+        for j in range(i, count):
+            r_ref[i * B : (i + 1) * B, j * B : (j + 1) * B] = shifted_block(
+                g_ref, i, j, count, row_count
+            )
 
     @pl.loop(0, count)
     def panel(k):
@@ -114,27 +354,31 @@
             )
 
 
-def cholesky(shifted):
-    width = shifted.shape[0]
+def cholesky(packed, width, row_count):
     return pl.pallas_call(
-        cholesky_kernel,
+        functools.partial(cholesky_kernel, row_count),
         out_shape=jax.ShapeDtypeStruct((width, width), F32),
         in_specs=[pl.BlockSpec(memory_space=pltpu.VMEM)],
         out_specs=pl.BlockSpec(memory_space=pltpu.VMEM),
         scratch_shapes=[
             pltpu.VMEM((6 * B, width), BF16),
             pltpu.VMEM((6 * B, width), BF16),
-            pltpu.VMEM((B, B), F32),
-            pltpu.VMEM((B, B), F32),
         ],
         compiler_params=pltpu.CompilerParams(vmem_limit_bytes=VMEM_LIMIT),
         name="cholesky",
-    )(shifted)
-
-
-def iterate_kernel(a_ref, x_ref, o_ref, hi_ref, mid_ref, low_ref):
+    )(packed)
+
+
+def iterate_kernel(row_count, g_ref, x_ref, o_ref, hi_ref, mid_ref, low_ref):
     width, modes = x_ref.shape
-    hi_ref[...], mid_ref[...], low_ref[...] = split3(a_ref[...])
+    count = width // B
+    for i in range(count):
+        for j in range(i, count):
+            block = shifted_block(g_ref, i, j, count, row_count)
+            a, b = slice(i * B, (i + 1) * B), slice(j * B, (j + 1) * B)
+            hi_ref[a, b], mid_ref[a, b], low_ref[a, b] = split3(block)
+            if i < j:
+                hi_ref[b, a], mid_ref[b, a], low_ref[b, a] = split3(block.T)
     o_ref[...] = x_ref[...]
 
     @pl.loop(0, ITERS)
@@ -163,17 +407,17 @@
         o_ref[...] = dot6(image, v, COLCOL)
 
 
-def iterate(shifted, start_block):
+def iterate(packed, start_block, row_count):
     width, modes = start_block.shape
     return pl.pallas_call(
-        iterate_kernel,
+        functools.partial(iterate_kernel, row_count),
         out_shape=jax.ShapeDtypeStruct((width, modes), F32),
         in_specs=[pl.BlockSpec(memory_space=pltpu.VMEM)] * 2,
         out_specs=pl.BlockSpec(memory_space=pltpu.VMEM),
         scratch_shapes=[pltpu.VMEM((width, width), BF16)] * 3,
         compiler_params=pltpu.CompilerParams(vmem_limit_bytes=VMEM_LIMIT),
         name="iterate",
-    )(shifted, start_block)
+    )(packed, start_block)
 
 
 def modes_kernel(m_ref, b_ref, o_ref):
@@ -204,21 +448,16 @@
 
 
 def body(snapshots, lengths, start_block):
-    snap = lax.axis_size("snap")
+    dofs, snap = lax.axis_size("dof"), lax.axis_size("snap")
     width = start_block.shape[0]
-    row_count = snapshots.shape[0] * lax.axis_size("dof")
-    own = lax.all_to_all(snapshots, "snap", split_axis=0, concat_axis=1, tiled=True)
-    active = active_columns(lengths, width)
-    masked = jnp.where(active[None, :], own, jnp.zeros_like(own))
-    gram = lax.psum(
-        lax.dot_general(masked, masked, COL0, preferred_element_type=F32), ("dof", "snap")
-    )
-    shifted = gram / F32(row_count) + 0.05 * jnp.eye(width, dtype=F32)
+    row_count = snapshots.shape[0] * dofs
+    active = jnp.broadcast_to(active_columns(lengths, width).astype(F32)[None, :], (8, width))
+    masked, packed = gram_of(snapshots, active, dofs, snap)
     first = lax.axis_index("snap") % 2 == 0
     upper, block = lax.cond(
         first,
-        lambda: (cholesky(shifted), start_block),
-        lambda: (shifted, iterate(shifted, start_block)),
+        lambda: (cholesky(packed, width, row_count), start_block),
+        lambda: (jnp.zeros((width, width), F32), iterate(packed, start_block, row_count)),
     )
     down = [(i, i + 1) for i in range(0, snap, 2)]
     up = [(i + 1, i) for i in range(0, snap, 2)]

time: 267 us -> 156 us (0.58)
  waiting for transfers between devices: 171 us -> 3.29 us
  Pallas kernels: 58.2 us -> 140 us
  between operations: 14.1 us -> 0.71 us
  matrix products: 4.38 us -> 0 us
  starting transfers between devices: 7.1 us -> 2.84 us
    psum x1 -> x0, waiting for transfers between devices: 143 us -> none  [body(): lax.psum(lax.dot_general(masked, masked, COL0, preferred_element_type=F32...]
    pallas_call x1 -> x2, Pallas kernels: 56.1 us -> 138 us  [the longest x1 79.7 us: gram_of(): pl.pallas_call(functools.partial(gram_kernel, dofs, snaps), out_shape=(ja...]
    all_to_all x1 -> x0, waiting for transfers between devices: 25.6 us -> none  [body(): lax.all_to_all(snapshots, 'snap', split_axis=0, concat_axis=1, tiled=True)]
    dot_general x1 -> x0, matrix products: 4.38 us -> none  [body(): lax.dot_general(masked, masked, COL0, preferred_element_type=F32)]
    all_to_all x1 -> x0, starting transfers between devices: 4.25 us -> none  [body(): lax.all_to_all(snapshots, 'snap', split_axis=0, concat_axis=1, tiled=True)]
    add x1 -> x0, other arithmetic: 3.04 us -> none  [body(): shifted = gram / F32(row_count) + 0.05 * jnp.eye(width, dtype=F32)]
  transfers between devices with their start and end apart: 4 -> 2, of which waited for: 4 -> 2; matrix products, arithmetic and copies ran while one was open for 0% -> 0% of each run, Pallas kernels for 1% -> 1%
where the time goes in v2:
time: 156 us
  Pallas kernels  140 us (90%)
  other arithmetic  6.37 us (4%)
  waiting for transfers between devices  3.29 us (2%)
  starting transfers between devices  2.84 us (2%)
  local copies, waits for them, and re-layouts  2.64 us (2%)
    pallas_call x1, Pallas kernels, gram_of(): pl.pallas_call(functools.partial(gram_kernel, dofs, snaps), out_shape=(ja...  79.7 us
    pallas_call x1, Pallas kernels, cholesky(): pl.pallas_call(functools.partial(cholesky_kernel, row_count), out_shape=j...  58.2 us
    select_n x1, other arithmetic, body(): upper = jnp.where(first, upper, lax.ppermute(upper, 'snap', down))  5.57 us
  transfers between devices with their start and end apart: 2, of which 2 were waited for; matrix products, arithmetic and copies ran while one was open for 0% of the time, Pallas kernels for 1%

profile of v2, /device:TPU:0, one launch (start us, length us, event | category | flops | bytes accessed | tf_op | source)
XLA Modules:
  0.0 156.0 jit_solution(11229600663215945705)
XLA Ops:
  0.7 0.7 select_reduce_fusion
  1.4 0.0 copy-start
  1.4 1.6 %copy-done = bf16[4096,256]{1,0:T(8,128)(2,1)S(1)} copy-done((bf16[4096,256]{1,0:T(8,128)(2,1)S(1)}, bf16[4096,256]{1,0:T(8,128)(2,1)}, u32[]{:S(2)}) %copy-start) | copy-done | bytes 2097176
  3.0 79.7 %gram.1 = (bf16[1024,1024]{1,0:T(8,128)(2,1)S(1)}, f32[4608,128]{1,0:T(8,128)S(1)}) custom-call(bf16[4096,256]{1,0:T(8,128)(2,1)S(1)} %copy-done, f32[8,1024]{1,0:T(8,128)S(1)} %broadcast_in_dim.23.active_ref), custom_call_target="tpu_custom_call" | custom-call | tf_op jit(solution)/shard_map/gram/pallas_call | solution.py:288
  82.7 59.4 %conditional.1 = (f32[1024,1024]{1,0:T(8,128)}, f32[1024,128]{1,0:T(8,128)S(1)}) conditional(s32[]{:T(128)} %convert_element_type.11, (f32[4608,128]{1,0:T(8,128)S(1)}, f32[1024,128]{1,0:T(8,128)}) %tuple.16, (f32[4608,128]{1,0:T(8,128)S(1)}, f32[1024,128]{1,0:T(8,128)}) %tuple.16), branch_computations={%region_1.2_spmd, %region_2.3_spmd} | conditional | bytes 4194324 | solution.py:457
  82.9 1.0 copy.8
  84.0 58.2 %cholesky.1 = f32[1024,1024]{1,0:T(8,128)} custom-call(f32[4608,128]{1,0:T(8,128)S(1)} %get-tuple-element.10.g_ref), custom_call_target="tpu_custom_call" | custom-call | tf_op jit(solution)/shard_map/cond/branch_1_fun/cholesky/pallas_call | solution.py:358
  142.2 1.5 collective-permute-start.1
  143.7 1.3 collective-permute-start
  145.0 2.5 %collective-permute-done = f32[1024,128]{1,0:T(8,128)S(1)} collective-permute-done((f32[1024,128]{1,0:T(8,128)S(1)}, f32[1024,128]{1,0:T(8,128)S(1)}, u32[]{:S(2)}, u32[]{:S(2)}) %collective-permute-start) | collective-permute-done | bytes 524320 | tf_op jit(solution)/shard_map/ppermute | solution.py:465
  147.5 0.1 broadcast_select_fusion.1.b_ref
  147.6 2.1 %modes.1 = f32[1024,128]{1,0:T(8,128)} custom-call(bf16[1024,1024]{1,0:T(8,128)(2,1)S(1)} %get-tuple-element.18.m_ref, f32[1024,128]{1,0:T(8,128)S(1)} %broadcast_select_fusion.1.b_ref), custom_call_target="tpu_custom_call" | custom-call | tf_op jit(solution)/shard_map/modes/pallas_call | solution.py:433
  149.6 0.8 collective-permute-done.1
  150.4 5.6 %broadcast_select_fusion = f32[1024,1024]{1,0:T(8,128)} fusion(f32[1024,1024]{1,0:T(8,128)} %get-tuple-element.21, f32[1024,1024]{1,0:T(8,128)S(1)} %collective-permute-done.1, pred[]{:T(512)S(6)} %eq.23), kind=kLoop, calls=%fused_computation | loop fusion | flops 1048576 | bytes 12582913 | tf_op jit(solution)/shard_map/jit(_where)/select_n | solution.py:464
  (3 shorter events, 0.0 us)
Async XLA Ops:
  1.4 1.6 %copy-start = (bf16[4096,256]{1,0:T(8,128)(2,1)S(1)}, bf16[4096,256]{1,0:T(8,128)(2,1)}, u32[]{:S(2)}) copy-start(bf16[4096,256]{1,0:T(8,128)(2,1)} %x_ref.1) | copy-start | bytes 6291460
  142.2 8.3 %collective-permute-start.1 = (f32[1024,1024]{1,0:T(8,128)}, f32[1024,1024]{1,0:T(8,128)S(1)}, u32[]{:S(2)}, u32[]{:S(2)}) collective-permute-start(f32[1024,1024]{1,0:T(8,128)} %get-tuple-element.21), channel_id=1, source_target_pairs={{0,1},{2,3},{4,5},{6,7},{8,9},{10,11},{12,13},{14,15},{16,17},{18,... | collective-permute-start | bytes 12582920 | tf_op jit(solution)/shard_map/ppermute | solution.py:464
  143.7 3.8 %collective-permute-start = (f32[1024,128]{1,0:T(8,128)S(1)}, f32[1024,128]{1,0:T(8,128)S(1)}, u32[]{:S(2)}, u32[]{:S(2)}) collective-permute-start(f32[1024,128]{1,0:T(8,128)S(1)} %get-tuple-element.20), channel_id=1, source_target_pairs={{1,0},{3,2},{5,4},{7,6},{9,8},{11,10},{13,12},{15,14},{17,16},{19,... | collective-permute-start | bytes 1572872 | tf_op jit(solution)/shard_map/ppermute | solution.py:465

commit v3 on v1

--- a/solution.py
+++ b/solution.py
@@ -88,10 +88,302 @@
     return jnp.where(c >= r, u, 0.0), v
 
 
-def cholesky_kernel(a_ref, r_ref, left_ref, right_ref, diag_ref, inv_ref):
-    width = a_ref.shape[0]
+MESH = pl.DeviceIdType.MESH
+
+
+def padded(blocks, devices):
+    return -(-blocks * B // (8 * devices)) * 8 * devices
+
+
+def layout(count, dofs):
+    half = count // 2
+    return padded(half * (half + 1) // 2, 2 * dofs), padded(half * half, 4 * dofs)
+
+
+def triangle(i, j, half):
+    return (i * half - i * (i - 1) // 2 + (j - i)) * B
+
+
+def block_rows(i, j, count, dofs):
+    half = count // 2
+    near, _ = layout(count, dofs)
+    if j < half:
+        return triangle(i, j, half)
+    if i >= half:
+        return near + triangle(i - half, j - half, half)
+    return 2 * near + (i * half + j - half) * B
+
+
+def radices_of(dofs):
+    found = []
+    left = dofs
+    while left > 1:
+        found.append(2 if not found else 4 if left % 4 == 0 else 2 if left % 2 == 0 else left)
+        left //= found[-1]
+    return found
+
+
+def far_stages(dofs, first):
+    d, s = lax.axis_index("dof"), lax.axis_index("snap")
+    stages, stride = [], 1
+    for n, radix in enumerate(radices_of(dofs)):
+        digit = (d // stride) % radix
+        if n >= first:
+            stages.append(
+                (
+                    digit,
+                    radix,
+                    lambda j, g=digit, r=radix, t=stride: (d + t * ((g + j) % r - g), s),
+                )
+            )
+        stride *= radix
+    return stages
+
+
+def gram_kernel(dofs, x_ref, active_ref, m_ref, g_ref, *scratch):
+    slots, extra, near_ref, part1, part2, diag, total, own_sems, send_sems, recv_sems = scratch[:10]
+    landing = list(scratch[10:])
+    d, s = lax.axis_index("dof"), lax.axis_index("snap")
+    core, y, x = s % 2, s // 2, d % 2
+    rest = 1 - core
+    rows, panel = slots.shape[1], slots.shape[2]
+    width = m_ref.shape[1]
     count = width // B
-    r_ref[...] = a_ref[...]
+    half = count // 2
+    near = part1.shape[0]
+    cross = part2.shape[0]
+    beside, over, across = s + 1 - 2 * core, (s + 2) % 4, (s + 1 - 2 * core + 2) % 4
+    pair = (core, 2, lambda j: (d, beside))
+    dof_stages = far_stages(dofs, 0)
+    stages1 = [pair] + dof_stages
+    stages2 = [
+        pair,
+        (
+            rest * x + core * y,
+            2,
+            lambda j: (d + rest * (1 - 2 * x), s + core * 2 * (1 - 2 * y)),
+        ),
+        (
+            rest * y + core * x,
+            2,
+            lambda j: (d + core * (1 - 2 * x), s + rest * 2 * (1 - 2 * y)),
+        ),
+    ] + dof_stages[1:]
+
+    greet = [(d, beside), (d, over), (d, across)]
+    for _, radix, peer in dof_stages:
+        greet += [peer(j) for j in range(1, radix)]
+    barrier = pltpu.get_barrier_semaphore()
+    for device in greet:
+        pl.semaphore_signal(barrier, inc=1, device_id=device, device_id_type=MESH)
+    pl.semaphore_wait(barrier, len(greet))
+
+    used = []
+
+    def send(src, dst, device):
+        n = len(used)
+        used.append(n)
+        copy = pltpu.make_async_remote_copy(
+            src_ref=src,
+            dst_ref=dst,
+            send_sem=send_sems.at[n],
+            recv_sem=recv_sems.at[n],
+            device_id=device,
+            device_id_type=MESH,
+        )
+        copy.start()
+        return copy
+
+    def quarter(q):
+        return x_ref.at[pl.ds(pl.multiple_of(q * rows, 16), rows), :]
+
+    def span(offset, size):
+        return pl.ds(pl.multiple_of(offset, 8), size)
+
+    def scatter(stages, part, put):
+        offset, length = 0, part.shape[0]
+        spans = []
+        for n, (digit, radix, peer) in enumerate(stages):
+            size = length // radix
+            arrive = landing.pop(0)
+            copies = [
+                send(
+                    part.at[span(offset + ((digit + j) % radix) * size, size), :],
+                    arrive.at[j - 1],
+                    peer(j),
+                )
+                for j in range(1, radix)
+            ]
+            offset, length = offset + digit * size, size
+            spans.append((offset, size))
+            for copy in copies:
+                copy.wait_recv()
+            value = part[span(offset, size), :]
+            for j in range(1, radix):
+                value = value + arrive[j - 1]
+            if n == len(stages) - 1:
+                put(span(offset, size), value)
+            else:
+                part[span(offset, size), :] = value
+            for copy in copies:
+                copy.wait_send()
+        return spans
+
+    def gather(stages, spans, view):
+        for n in reversed(range(len(stages))):
+            _, radix, peer = stages[n]
+            here = view(span(*spans[n]))
+            copies = [send(here, here, peer(j)) for j in range(1, radix)]
+            for copy in copies:
+                copy.wait_recv()
+            for copy in copies:
+                copy.wait_send()
+
+    pair_copies = [
+        send(quarter(beside), slots.at[s], (d, beside)),
+        send(quarter(across), extra.at[core], (d, beside)),
+    ]
+    far_copies = [
+        send(quarter(over), slots.at[s], (d, over)),
+        send(quarter(across), slots.at[s], (d, across)),
+    ]
+    own = [
+        pltpu.make_async_copy(quarter(s), slots.at[s], own_sems.at[0]),
+        pltpu.make_async_copy(quarter(over), extra.at[core], own_sems.at[1]),
+    ]
+    for copy in own:
+        copy.start()
+    for copy in own:
+        copy.wait()
+    for copy in pair_copies:
+        copy.wait_recv()
+
+    for i in range(2):
+        columns = slice(i * panel, (i + 1) * panel)
+        q = 2 * y + i
+        keep = active_ref[0:1, pl.ds(pl.multiple_of(q * panel, panel), panel)]
+        near_ref[:rows, columns] = (slots[q].astype(F32) * keep).astype(BF16)
+        near_ref[rows:, columns] = (extra[i].astype(F32) * keep).astype(BF16)
+    for i in range(half):
+        strip = lax.dot_general(
+            near_ref[:, i * B : (i + 1) * B],
+            near_ref[:, i * B :],
+            COL0,
+            preferred_element_type=F32,
+        )
+        for j in range(i, half):
+            first = triangle(i, j, half)
+            part1[first : first + B, :] = strip[:, (j - i) * B : (j - i + 1) * B]
+    end = half * (half + 1) // 2 * B
+    if end < near:
+        part1[end:, :] = jnp.zeros((near - end, B), F32)
+
+    def put_diag(here, value):
+        diag[y, here, :] = value
+
+    spans = scatter(stages1, part1, put_diag)
+    gather(stages1, spans, lambda here: diag.at[y, here, :])
+    mine = span(core * (near // 2), near // 2)
+    swap = send(diag.at[y, mine, :], diag.at[y, mine, :], (d, over))
+
+    for copy in far_copies:
+        copy.wait_recv()
+    for i in range(4):
+        columns = slice(i * panel, (i + 1) * panel)
+        m_ref[:, columns] = (
+            slots[i].astype(F32) * active_ref[0:1, columns]
+        ).astype(BF16)
+    for i in range(half):
+        strip = lax.dot_general(
+            m_ref[:, i * B : (i + 1) * B],
+            m_ref[:, half * B :],
+            COL0,
+            preferred_element_type=F32,
+        )
+        for j in range(half):
+            first = (i * half + j) * B
+            part2[first : first + B, :] = strip[:, j * B : (j + 1) * B]
+    end = half * half * B
+    if end < cross:
+        part2[end:, :] = jnp.zeros((cross - end, B), F32)
+
+    def put_total(here, value):
+        total[here, :] = value
+
+    spans = scatter(stages2, part2, put_total)
+    swap.wait_recv()
+    other = diag.at[1 - y, mine, :]
+    share = send(other, other, (d, beside))
+    gather(stages2, spans, lambda here: total.at[here, :])
+    share.wait_recv()
+    g_ref[:near, :] = diag[0]
+    g_ref[near : 2 * near, :] = diag[1]
+    g_ref[2 * near :, :] = total[...]
+    for copy in [*pair_copies, *far_copies, swap, share]:
+        copy.wait_send()
+
+
+def gram_of(snapshots, active, dofs, snaps):
+    rows, panel = snapshots.shape[0] // snaps, snapshots.shape[1]
+    width = panel * snaps
+    near, cross = layout(width // B, dofs)
+    far = radices_of(dofs)
+    landing, copies = [], 6
+    for radices, length in (([2] + far, near), ([2, 2] + far, cross)):
+        for radix in radices:
+            length //= radix
+            landing.append(pltpu.VMEM((radix - 1, length, B), F32))
+            copies += 2 * (radix - 1)
+    return pl.pallas_call(
+        functools.partial(gram_kernel, dofs),
+        out_shape=(
+            jax.ShapeDtypeStruct((rows, width), BF16),
+            jax.ShapeDtypeStruct((2 * near + cross, B), F32),
+        ),
+        in_specs=[
+            pl.BlockSpec(memory_space=pl.ANY),
+            pl.BlockSpec(memory_space=pltpu.VMEM),
+        ],
+        out_specs=(pl.BlockSpec(memory_space=pltpu.VMEM),) * 2,
+        scratch_shapes=[
+            pltpu.VMEM((snaps, rows, panel), BF16),
+            pltpu.VMEM((2, rows, panel), BF16),
+            pltpu.VMEM((2 * rows, 2 * panel), BF16),
+            pltpu.VMEM((near, B), F32),
+            pltpu.VMEM((cross, B), F32),
+            pltpu.VMEM((2, near, B), F32),
+            pltpu.VMEM((cross, B), F32),
+            pltpu.SemaphoreType.DMA((2,)),
+            pltpu.SemaphoreType.DMA((copies,)),
+            pltpu.SemaphoreType.DMA((copies,)),
+            *landing,
+        ],
+        compiler_params=pltpu.CompilerParams(
+            collective_id=0, has_side_effects=True, vmem_limit_bytes=VMEM_LIMIT
+        ),
+        name="gram",
+    )(snapshots, active)
+
+
+def shifted_block(g_ref, i, j, count, dofs, row_count):
+    first = block_rows(i, j, count, dofs)
+    block = g_ref[first : first + B, :] / F32(row_count)
+    if i == j:
+        r = lax.broadcasted_iota(jnp.int32, (B, B), 0)
+        c = lax.broadcasted_iota(jnp.int32, (B, B), 1)
+        block = block + jnp.where(r == c, 0.05, 0.0).astype(F32)
+    return block
+
+
+def cholesky_kernel(dofs, row_count, g_ref, r_ref, left_ref, right_ref):
+    width = r_ref.shape[0]
+    count = width // B
+    for i in range(count):
+        r_ref[i * B : (i + 1) * B, :] = jnp.zeros((B, width), F32)
+        for j in range(i, count):
+            r_ref[i * B : (i + 1) * B, j * B : (j + 1) * B] = shifted_block(
+                g_ref, i, j, count, dofs, row_count
+            )
 
     @pl.loop(0, count)
     def panel(k):
@@ -114,27 +406,31 @@
             )
 
 
-def cholesky(shifted):
-    width = shifted.shape[0]
+def cholesky(packed, width, dofs, row_count):
     return pl.pallas_call(
-        cholesky_kernel,
+        functools.partial(cholesky_kernel, dofs, row_count),
         out_shape=jax.ShapeDtypeStruct((width, width), F32),
         in_specs=[pl.BlockSpec(memory_space=pltpu.VMEM)],
         out_specs=pl.BlockSpec(memory_space=pltpu.VMEM),
         scratch_shapes=[
             pltpu.VMEM((6 * B, width), BF16),
             pltpu.VMEM((6 * B, width), BF16),
-            pltpu.VMEM((B, B), F32),
-            pltpu.VMEM((B, B), F32),
         ],
         compiler_params=pltpu.CompilerParams(vmem_limit_bytes=VMEM_LIMIT),
         name="cholesky",
-    )(shifted)
-
-
-def iterate_kernel(a_ref, x_ref, o_ref, hi_ref, mid_ref, low_ref):
+    )(packed)
+
+
+def iterate_kernel(dofs, row_count, g_ref, x_ref, o_ref, hi_ref, mid_ref, low_ref):
     width, modes = x_ref.shape
-    hi_ref[...], mid_ref[...], low_ref[...] = split3(a_ref[...])
+    count = width // B
+    for i in range(count):
+        for j in range(i, count):
+            block = shifted_block(g_ref, i, j, count, dofs, row_count)
+            a, b = slice(i * B, (i + 1) * B), slice(j * B, (j + 1) * B)
+            hi_ref[a, b], mid_ref[a, b], low_ref[a, b] = split3(block)
+            if i < j:
+                hi_ref[b, a], mid_ref[b, a], low_ref[b, a] = split3(block.T)
     o_ref[...] = x_ref[...]
 
     @pl.loop(0, ITERS)
@@ -163,17 +459,17 @@
         o_ref[...] = dot6(image, v, COLCOL)
 
 
-def iterate(shifted, start_block):
+def iterate(packed, start_block, dofs, row_count):
     width, modes = start_block.shape
     return pl.pallas_call(
-        iterate_kernel,
+        functools.partial(iterate_kernel, dofs, row_count),
         out_shape=jax.ShapeDtypeStruct((width, modes), F32),
         in_specs=[pl.BlockSpec(memory_space=pltpu.VMEM)] * 2,
         out_specs=pl.BlockSpec(memory_space=pltpu.VMEM),
         scratch_shapes=[pltpu.VMEM((width, width), BF16)] * 3,
         compiler_params=pltpu.CompilerParams(vmem_limit_bytes=VMEM_LIMIT),
         name="iterate",
-    )(shifted, start_block)
+    )(packed, start_block)
 
 
 def modes_kernel(m_ref, b_ref, o_ref):
@@ -204,21 +500,16 @@
 
 
 def body(snapshots, lengths, start_block):
-    snap = lax.axis_size("snap")
+    dofs, snap = lax.axis_size("dof"), lax.axis_size("snap")
     width = start_block.shape[0]
-    row_count = snapshots.shape[0] * lax.axis_size("dof")
-    own = lax.all_to_all(snapshots, "snap", split_axis=0, concat_axis=1, tiled=True)
-    active = active_columns(lengths, width)
-    masked = jnp.where(active[None, :], own, jnp.zeros_like(own))
-    gram = lax.psum(
-        lax.dot_general(masked, masked, COL0, preferred_element_type=F32), ("dof", "snap")
-    )
-    shifted = gram / F32(row_count) + 0.05 * jnp.eye(width, dtype=F32)
+    row_count = snapshots.shape[0] * dofs
+    active = jnp.broadcast_to(active_columns(lengths, width).astype(F32)[None, :], (8, width))
+    masked, packed = gram_of(snapshots, active, dofs, snap)
     first = lax.axis_index("snap") % 2 == 0
     upper, block = lax.cond(
         first,
-        lambda: (cholesky(shifted), start_block),
-        lambda: (shifted, iterate(shifted, start_block)),
+        lambda: (cholesky(packed, width, dofs, row_count), start_block),
+        lambda: (jnp.zeros((width, width), F32), iterate(packed, start_block, dofs, row_count)),
     )
     down = [(i, i + 1) for i in range(0, snap, 2)]
     up = [(i + 1, i) for i in range(0, snap, 2)]

time: 267 us -> 141 us (0.53)
  waiting for transfers between devices: 171 us -> 3.29 us
  Pallas kernels: 58.2 us -> 124 us
  between operations: 14.1 us -> 0.71 us
  matrix products: 4.38 us -> 0 us
  starting transfers between devices: 7.1 us -> 2.84 us
    psum x1 -> x0, waiting for transfers between devices: 143 us -> none  [body(): lax.psum(lax.dot_general(masked, masked, COL0, preferred_element_type=F32...]
    pallas_call x1 -> x2, Pallas kernels: 56.1 us -> 122 us  [the longest x1 64.1 us: gram_of(): pl.pallas_call(functools.partial(gram_kernel, dofs), out_shape=(jax.Shape...]
    all_to_all x1 -> x0, waiting for transfers between devices: 25.6 us -> none  [body(): lax.all_to_all(snapshots, 'snap', split_axis=0, concat_axis=1, tiled=True)]
    dot_general x1 -> x0, matrix products: 4.38 us -> none  [body(): lax.dot_general(masked, masked, COL0, preferred_element_type=F32)]
    all_to_all x1 -> x0, starting transfers between devices: 4.25 us -> none  [body(): lax.all_to_all(snapshots, 'snap', split_axis=0, concat_axis=1, tiled=True)]
    add x1 -> x0, other arithmetic: 3.04 us -> none  [body(): shifted = gram / F32(row_count) + 0.05 * jnp.eye(width, dtype=F32)]
  transfers between devices with their start and end apart: 4 -> 2, of which waited for: 4 -> 2; matrix products, arithmetic and copies ran while one was open for 0% -> 0% of each run, Pallas kernels for 1% -> 1%
where the time goes in v3:
time: 141 us; the launch traced here: 140 us
  Pallas kernels  124 us (88%)
  other arithmetic  6.37 us (5%)
  waiting for transfers between devices  3.29 us (2%)
  starting transfers between devices  2.84 us (2%)
  local copies, waits for them, and re-layouts  2.64 us (2%)
    pallas_call x1, Pallas kernels, gram_of(): pl.pallas_call(functools.partial(gram_kernel, dofs), out_shape=(jax.Shape...  64.1 us
    pallas_call x1, Pallas kernels, cholesky(): pl.pallas_call(functools.partial(cholesky_kernel, dofs, row_count), out_s...  58.2 us
    select_n x1, other arithmetic, body(): upper = jnp.where(first, upper, lax.ppermute(upper, 'snap', down))  5.57 us
  transfers between devices with their start and end apart: 2, of which 2 were waited for; matrix products, arithmetic and copies ran while one was open for 0% of the time, Pallas kernels for 1%

profile of v3, /device:TPU:0, one launch (start us, length us, event | category | flops | bytes accessed | tf_op | source)
XLA Modules:
  0.0 140.4 jit_solution(6893778616050218172)
XLA Ops:
  0.7 0.7 select_reduce_fusion
  1.4 0.0 copy-start
  1.4 1.6 %copy-done = bf16[4096,256]{1,0:T(8,128)(2,1)S(1)} copy-done((bf16[4096,256]{1,0:T(8,128)(2,1)S(1)}, bf16[4096,256]{1,0:T(8,128)(2,1)}, u32[]{:S(2)}) %copy-start) | copy-done | bytes 2097176
  3.0 64.1 %gram.1 = (bf16[1024,1024]{1,0:T(8,128)(2,1)S(1)}, f32[4608,128]{1,0:T(8,128)S(1)}) custom-call(bf16[4096,256]{1,0:T(8,128)(2,1)S(1)} %copy-done, f32[8,1024]{1,0:T(8,128)S(1)} %broadcast_in_dim.23.active_ref), custom_call_target="tpu_custom_call" | custom-call | tf_op jit(solution)/shard_map/gram/pallas_call | solution.py:337
  67.2 59.4 %conditional.1 = (f32[1024,1024]{1,0:T(8,128)}, f32[1024,128]{1,0:T(8,128)S(1)}) conditional(s32[]{:T(128)} %convert_element_type.11, (f32[4608,128]{1,0:T(8,128)S(1)}, f32[1024,128]{1,0:T(8,128)}) %tuple.16, (f32[4608,128]{1,0:T(8,128)S(1)}, f32[1024,128]{1,0:T(8,128)}) %tuple.16), branch_computations={%region_1.2_spmd, %region_2.3_spmd} | conditional | bytes 4194324 | solution.py:509
  67.4 1.0 copy.8
  68.4 58.2 %cholesky.1 = f32[1024,1024]{1,0:T(8,128)} custom-call(f32[4608,128]{1,0:T(8,128)S(1)} %get-tuple-element.10.g_ref), custom_call_target="tpu_custom_call" | custom-call | tf_op jit(solution)/shard_map/cond/branch_1_fun/cholesky/pallas_call | solution.py:410
  126.6 1.5 %collective-permute-start.1 = (f32[1024,1024]{1,0:T(8,128)}, f32[1024,1024]{1,0:T(8,128)S(1)}, u32[]{:S(2)}, u32[]{:S(2)}) collective-permute-start(f32[1024,1024]{1,0:T(8,128)} %get-tuple-element.21), channel_id=1, source_target_pairs={{0,1},{2,3},{4,5},{6,7},{8,9},{10,11},{12,13},{14,15},{16,17},{18,... | collective-permute-start | bytes 12582920 | tf_op jit(solution)/shard_map/ppermute | solution.py:516
  128.1 1.3 collective-permute-start
  129.4 2.5 %collective-permute-done = f32[1024,128]{1,0:T(8,128)S(1)} collective-permute-done((f32[1024,128]{1,0:T(8,128)S(1)}, f32[1024,128]{1,0:T(8,128)S(1)}, u32[]{:S(2)}, u32[]{:S(2)}) %collective-permute-start) | collective-permute-done | bytes 524320 | tf_op jit(solution)/shard_map/ppermute | solution.py:517
  131.9 0.1 broadcast_select_fusion.1.b_ref
  132.0 2.1 %modes.1 = f32[1024,128]{1,0:T(8,128)} custom-call(bf16[1024,1024]{1,0:T(8,128)(2,1)S(1)} %get-tuple-element.18.m_ref, f32[1024,128]{1,0:T(8,128)S(1)} %broadcast_select_fusion.1.b_ref), custom_call_target="tpu_custom_call" | custom-call | tf_op jit(solution)/shard_map/modes/pallas_call | solution.py:485
  134.1 0.8 collective-permute-done.1
  134.8 5.6 %broadcast_select_fusion = f32[1024,1024]{1,0:T(8,128)} fusion(f32[1024,1024]{1,0:T(8,128)} %get-tuple-element.21, f32[1024,1024]{1,0:T(8,128)S(1)} %collective-permute-done.1, pred[]{:T(512)S(6)} %eq.23), kind=kLoop, calls=%fused_computation | loop fusion | flops 1048576 | bytes 12582913 | tf_op jit(solution)/shard_map/jit(_where)/select_n | solution.py:516
  (3 shorter events, 0.0 us)
Async XLA Ops:
  1.4 1.6 %copy-start = (bf16[4096,256]{1,0:T(8,128)(2,1)S(1)}, bf16[4096,256]{1,0:T(8,128)(2,1)}, u32[]{:S(2)}) copy-start(bf16[4096,256]{1,0:T(8,128)(2,1)} %x_ref.1) | copy-start | bytes 6291460
  126.6 8.3 %collective-permute-start.1 = (f32[1024,1024]{1,0:T(8,128)}, f32[1024,1024]{1,0:T(8,128)S(1)}, u32[]{:S(2)}, u32[]{:S(2)}) collective-permute-start(f32[1024,1024]{1,0:T(8,128)} %get-tuple-element.21), channel_id=1, source_target_pairs={{0,1},{2,3},{4,5},{6,7},{8,9},{10,11},{12,13},{14,15},{16,17},{18,... | collective-permute-start | bytes 12582920 | tf_op jit(solution)/shard_map/ppermute | solution.py:516
  128.1 3.8 %collective-permute-start = (f32[1024,128]{1,0:T(8,128)S(1)}, f32[1024,128]{1,0:T(8,128)S(1)}, u32[]{:S(2)}, u32[]{:S(2)}) collective-permute-start(f32[1024,128]{1,0:T(8,128)S(1)} %get-tuple-element.20), channel_id=1, source_target_pairs={{1,0},{3,2},{5,4},{7,6},{9,8},{11,10},{13,12},{15,14},{17,16},{19,... | collective-permute-start | bytes 1572872 | tf_op jit(solution)/shard_map/ppermute | solution.py:517

commit v4 on v3

--- a/solution.py
+++ b/solution.py
@@ -11,6 +11,7 @@
 ITERS = 3
 PASSES = 16
 B = 128
+G = 16
 VMEM_LIMIT = 48 * 1024 * 1024
 F32 = jnp.float32
 BF16 = jnp.bfloat16
@@ -34,50 +35,50 @@
 
 
 def factor_block(block):
-    rows = [None] * (B // 8)
-    for i in range(B // 8):
-        r = lax.broadcasted_iota(jnp.int32, (8, B), 0) + 8 * i
-        c = lax.broadcasted_iota(jnp.int32, (8, B), 1)
-        rows[i] = (block[8 * i : 8 * i + 8, :], jnp.where(r == c, 1.0, 0.0).astype(F32))
-    sub = lax.broadcasted_iota(jnp.int32, (8, B), 0)
+    rows = [None] * (B // G)
+    for i in range(B // G):
+        r = lax.broadcasted_iota(jnp.int32, (G, B), 0) + G * i
+        c = lax.broadcasted_iota(jnp.int32, (G, B), 1)
+        rows[i] = (block[G * i : G * i + G, :], jnp.where(r == c, 1.0, 0.0).astype(F32))
+    sub = lax.broadcasted_iota(jnp.int32, (G, B), 0)
     upper, inverse = [], []
-    for g in range(B // 8):
+    for g in range(B // G):
         left, right = rows[g]
         cols = [
-            jnp.broadcast_to(left[:, 8 * g + t : 8 * g + t + 1], (8, B)) for t in range(8)
+            jnp.broadcast_to(left[:, G * g + t : G * g + t + 1], (G, B)) for t in range(G)
         ]
         outer = [
             [
-                jnp.broadcast_to(rows[i][0][:, 8 * g + t : 8 * g + t + 1], (8, B))
-                for t in range(8)
+                jnp.broadcast_to(rows[i][0][:, G * g + t : G * g + t + 1], (G, B))
+                for t in range(G)
             ]
-            for i in range(g + 1, B // 8)
+            for i in range(g + 1, B // G)
         ]
-        u_tile = jnp.zeros((8, B), F32)
-        v_tile = jnp.zeros((8, B), F32)
-        for t in range(8):
-            pivot = jnp.broadcast_to(cols[t][t : t + 1, :], (8, B))
+        u_tile = jnp.zeros((G, B), F32)
+        v_tile = jnp.zeros((G, B), F32)
+        for t in range(G):
+            pivot = jnp.broadcast_to(cols[t][t : t + 1, :], (G, B))
             recip = 1.0 / pivot
             scale = lax.rsqrt(pivot)
-            left_row = jnp.broadcast_to(left[t : t + 1, :], (8, B))
-            right_row = jnp.broadcast_to(right[t : t + 1, :], (8, B))
+            left_row = jnp.broadcast_to(left[t : t + 1, :], (G, B))
+            right_row = jnp.broadcast_to(right[t : t + 1, :], (G, B))
             u_tile = jnp.where(sub == t, left_row * scale, u_tile)
             v_tile = jnp.where(sub == t, right_row * scale, v_tile)
             factor = jnp.where(sub == t, cols[t] - 1.0, cols[t]) * recip
             left_new = jnp.where(sub == t, left_row * recip, left - factor * left_row)
             right_new = jnp.where(sub == t, right_row * recip, right - factor * right_row)
-            for c in range(t + 1, 8):
-                head = jnp.broadcast_to(cols[c][t : t + 1, :], (8, B))
+            for c in range(t + 1, G):
+                head = jnp.broadcast_to(cols[c][t : t + 1, :], (G, B))
                 cols[c] = jnp.where(sub == t, head * recip, cols[c] - factor * head)
             left, right = left_new, right_new
         upper.append(u_tile)
         inverse.append(v_tile)
-        left_rows = [jnp.broadcast_to(left[t : t + 1, :], (8, B)) for t in range(8)]
-        right_rows = [jnp.broadcast_to(right[t : t + 1, :], (8, B)) for t in range(8)]
-        for i in range(g + 1, B // 8):
+        left_rows = [jnp.broadcast_to(left[t : t + 1, :], (G, B)) for t in range(G)]
+        right_rows = [jnp.broadcast_to(right[t : t + 1, :], (G, B)) for t in range(G)]
+        for i in range(g + 1, B // G):
             a, b = rows[i]
             coef = outer[i - g - 1]
-            for t in range(8):
+            for t in range(G):
                 a = a - coef[t] * left_rows[t]
                 b = b - coef[t] * right_rows[t]
             rows[i] = (a, b)
@@ -421,8 +422,10 @@
     )(packed)
 
 
-def iterate_kernel(dofs, row_count, g_ref, x_ref, o_ref, hi_ref, mid_ref, low_ref):
+def iterate_kernel(dofs, row_count, g_ref, x_ref, full_ref, hi_ref, mid_ref, low_ref):
     width, modes = x_ref.shape
+    o_ref = full_ref.at[:, :modes]
+    full_ref[:, modes:] = jnp.zeros((width, width - modes), F32)
     count = width // B
     for i in range(count):
         for j in range(i, count):
@@ -463,7 +466,7 @@
     width, modes = start_block.shape
     return pl.pallas_call(
         functools.partial(iterate_kernel, dofs, row_count),
-        out_shape=jax.ShapeDtypeStruct((width, modes), F32),
+        out_shape=jax.ShapeDtypeStruct((width, width), F32),
         in_specs=[pl.BlockSpec(memory_space=pltpu.VMEM)] * 2,
         out_specs=pl.BlockSpec(memory_space=pltpu.VMEM),
         scratch_shapes=[pltpu.VMEM((width, width), BF16)] * 3,
@@ -472,24 +475,59 @@
     )(packed, start_block)
 
 
-def modes_kernel(m_ref, b_ref, o_ref):
-    modes = b_ref.shape[1]
-    b1, b2, b3 = split3(b_ref[...])
-    parts = lax.dot_general(
-        m_ref[...], jnp.concatenate([b1, b2, b3], axis=1), ROWCOL, preferred_element_type=F32
-    )
-    o_ref[...] = (parts[:, 2 * modes :] + parts[:, modes : 2 * modes]) + parts[:, :modes]
-
-
-def modes_of(masked, block):
+def finish_kernel(first_ref, mine_ref, got_ref, m_ref, o_ref, r_ref, block_ref, sems):
+    modes = o_ref.shape[1]
+    first = first_ref[0] == 1
+
+    def finish(r_source, b_source):
+        factor = pltpu.make_async_copy(r_source, r_ref, sems.at[0])
+        block = pltpu.make_async_copy(b_source.at[:, :modes], block_ref, sems.at[1])
+        block.start()
+        factor.start()
+        block.wait()
+        b1, b2, b3 = split3(block_ref[...])
+        parts = lax.dot_general(
+            m_ref[...],
+            jnp.concatenate([b1, b2, b3], axis=1),
+            ROWCOL,
+            preferred_element_type=F32,
+        )
+        o_ref[...] = (parts[:, 2 * modes :] + parts[:, modes : 2 * modes]) + parts[:, :modes]
+        factor.wait()
+
+    @pl.when(first)
+    def _():
+        finish(mine_ref, got_ref)
+
+    @pl.when(jnp.logical_not(first))
+    def _():
+        finish(got_ref, mine_ref)
+
+
+def finish_of(first, mine, got, masked, modes):
     return pl.pallas_call(
-        modes_kernel,
-        out_shape=jax.ShapeDtypeStruct((masked.shape[0], block.shape[1]), F32),
-        in_specs=[pl.BlockSpec(memory_space=pltpu.VMEM)] * 2,
-        out_specs=pl.BlockSpec(memory_space=pltpu.VMEM),
-        compiler_params=pltpu.CompilerParams(vmem_limit_bytes=VMEM_LIMIT),
-        name="modes",
-    )(masked, block)
+        finish_kernel,
+        out_shape=(
+            jax.ShapeDtypeStruct((masked.shape[0], modes), F32),
+            jax.ShapeDtypeStruct(mine.shape, F32),
+        ),
+        in_specs=[
+            pl.BlockSpec(memory_space=pltpu.SMEM),
+            pl.BlockSpec(memory_space=pl.ANY),
+            pl.BlockSpec(memory_space=pl.ANY),
+            pl.BlockSpec(memory_space=pltpu.VMEM),
+        ],
+        out_specs=(
+            pl.BlockSpec(memory_space=pltpu.VMEM),
+            pl.BlockSpec(memory_space=pl.ANY),
+        ),
+        scratch_shapes=[
+            pltpu.VMEM((mine.shape[0], modes), F32),
+            pltpu.SemaphoreType.DMA((2,)),
+        ],
+        compiler_params=pltpu.CompilerParams(vmem_limit_bytes=VMEM_LIMIT // 2),
+        name="finish",
+    )(first, mine, got, masked)
 
 
 def active_columns(lengths, width):
@@ -506,16 +544,13 @@
     active = jnp.broadcast_to(active_columns(lengths, width).astype(F32)[None, :], (8, width))
     masked, packed = gram_of(snapshots, active, dofs, snap)
     first = lax.axis_index("snap") % 2 == 0
-    upper, block = lax.cond(
+    mine = lax.cond(
         first,
-        lambda: (cholesky(packed, width, dofs, row_count), start_block),
-        lambda: (jnp.zeros((width, width), F32), iterate(packed, start_block, dofs, row_count)),
+        lambda: cholesky(packed, width, dofs, row_count),
+        lambda: iterate(packed, start_block, dofs, row_count),
     )
-    down = [(i, i + 1) for i in range(0, snap, 2)]
-    up = [(i + 1, i) for i in range(0, snap, 2)]
-    upper = jnp.where(first, upper, lax.ppermute(upper, "snap", down))
-    block = jnp.where(first, lax.ppermute(block, "snap", up), block)
-    return modes_of(masked, block), upper
+    got = lax.ppermute(mine, "snap", [(i, i + 1 - 2 * (i % 2)) for i in range(snap)])
+    return finish_of(first.astype(jnp.int32).reshape(1), mine, got, masked, start_block.shape[1])
 
 
 def solution(mesh):

time: 141 us -> 254 us (1.80)
  Pallas kernels: 124 us -> 243 us
  other arithmetic: 6.37 us -> 0.75 us
  waiting for transfers between devices: 3.29 us -> 7.37 us
  starting transfers between devices: 2.84 us -> 0.01 us
    pallas_call x1, Pallas kernels: 2.06 us -> 129 us  [finish_of(): pl.pallas_call(finish_kernel, out_shape=(jax.ShapeDtypeStruct((masked.sha...]
    pallas_call x1, Pallas kernels: 58.2 us -> 50.1 us  [cholesky(): pl.pallas_call(functools.partial(cholesky_kernel, dofs, row_count), out_s...]
    select_n x2 -> x0, other arithmetic: 5.63 us -> none  [the longest x1 5.57 us: body(): upper = jnp.where(first, upper, lax.ppermute(upper, 'snap', down))]
    ppermute x2 -> x1, waiting for transfers between devices: 3.29 us -> 7.37 us  [body(): lax.ppermute(mine, 'snap', [(i, i + 1 - 2 * (i % 2)) for i in range(snap)])]
    ppermute x2 -> x1, starting transfers between devices: 2.84 us -> 0.01 us  [body(): lax.ppermute(mine, 'snap', [(i, i + 1 - 2 * (i % 2)) for i in range(snap)])]
  transfers between devices with their start and end apart: 2 -> 1, of which waited for: 2 -> 1; matrix products, arithmetic and copies ran while one was open for 0% -> 0% of each run, Pallas kernels for 1% -> 0%
where the time goes in v4:
time: 254 us
  Pallas kernels  243 us (96%)
  waiting for transfers between devices  7.37 us (3%)
    pallas_call x1, Pallas kernels, finish_of(): pl.pallas_call(finish_kernel, out_shape=(jax.ShapeDtypeStruct((masked.sha...  129 us
    pallas_call x1, Pallas kernels, gram_of(): pl.pallas_call(functools.partial(gram_kernel, dofs), out_shape=(jax.Shape...  64.2 us
    pallas_call x1, Pallas kernels, cholesky(): pl.pallas_call(functools.partial(cholesky_kernel, dofs, row_count), out_s...  50.1 us
    ppermute x1, waiting for transfers between devices, body(): lax.ppermute(mine, 'snap', [(i, i + 1 - 2 * (i % 2)) for i in range(snap)])  7.37 us
  transfers between devices with their start and end apart: 1, of which 1 were waited for; matrix products, arithmetic and copies ran while one was open for 0% of the time, Pallas kernels for 0%

profile of v4, /device:TPU:0, one launch (start us, length us, event | category | flops | bytes accessed | tf_op | source)
XLA Modules:
  0.0 254.1 jit_solution(17301881663511759013)
XLA Ops:
  0.7 0.7 select_reduce_fusion
  1.4 0.0 copy-start
  1.4 1.6 copy-done
  3.0 64.2 %gram.1 = (bf16[1024,1024]{1,0:T(8,128)(2,1)S(1)}, f32[4608,128]{1,0:T(8,128)S(1)}) custom-call(bf16[4096,256]{1,0:T(8,128)(2,1)S(1)} %copy-done, f32[8,1024]{1,0:T(8,128)S(1)} %broadcast_in_dim.23.active_ref), custom_call_target="tpu_custom_call" | custom-call | tf_op jit(solution)/shard_map/gram/pallas_call | solution.py:338
  67.2 50.3 %conditional.1 = (f32[1024,1024]{1,0:T(8,128)}) conditional(s32[]{:T(128)} %convert_element_type.11, (f32[4608,128]{1,0:T(8,128)S(1)}, f32[1024,128]{1,0:T(8,128)}) %tuple.13, f32[4608,128]{1,0:T(8,128)S(1)} %get-tuple-element.14), branch_computations={%region_1.2_spmd, %region_2.3_spmd} | conditional | bytes 8 | solution.py:547
  67.4 50.1 %cholesky.1 = f32[1024,1024]{1,0:T(8,128)} custom-call(f32[4608,128]{1,0:T(8,128)S(1)} %g_ref), custom_call_target="tpu_custom_call" | custom-call | tf_op jit(solution)/shard_map/cond/branch_1_fun/cholesky/pallas_call | solution.py:411
  117.6 0.0 collective-permute-start
  117.6 7.4 %collective-permute-done.got_ref = f32[1024,1024]{1,0:T(8,128)S(1)} collective-permute-done((f32[1024,1024]{1,0:T(8,128)}, f32[1024,1024]{1,0:T(8,128)S(1)}, u32[]{:S(2)}, u32[]{:S(2)}) %collective-permute-start) | collective-permute-done | bytes 4194336 | tf_op jit(solution)/shard_map/ppermute | solution.py:552
  124.9 129.0 %finish.1 = (f32[1024,128]{1,0:T(8,128)}, f32[1024,1024]{1,0:T(8,128)}) custom-call(s32[1]{0:T(128)} %bitcast.first_ref, f32[1024,1024]{1,0:T(8,128)} %get-tuple-element.18.mine_ref, f32[1024,1024]{1,0:T(8,128)S(1)} %collective-permute-done.got_ref, bf16[1024,1024]{1,0:T(8,128)(2,1)S(1)} %get-tuple-element.15.m_ref), custom_call_target="tpu_custom_call" | custom-call | tf_op jit(solution)/shard_map/finish/pallas_call | solution.py:508
  (3 shorter events, 0.0 us)
Async XLA Ops:
  1.4 1.6 copy-start
  117.6 7.4 %collective-permute-start = (f32[1024,1024]{1,0:T(8,128)}, f32[1024,1024]{1,0:T(8,128)S(1)}, u32[]{:S(2)}, u32[]{:S(2)}) collective-permute-start(f32[1024,1024]{1,0:T(8,128)} %get-tuple-element.18.mine_ref), channel_id=1, source_target_pairs={{0,1},{1,0},{2,3},{3,2},{4,5},{5,4},{6,7},{7,6},{8,9},{9,8},{10,11... | collective-permute-start | bytes 12582920 | tf_op jit(solution)/shard_map/ppermute | solution.py:552
